TPU v7x, 32 devices: a whole 2x2x4 slice. The times are simulated.
32 devices in a mesh: surveys: 2 (over y), tx: 4 (over z), ty: 4 (over x, core).
Axes of the slice: x: 2, y: 2, z: 4, core: 2. Of those that a mesh axis runs over, the one named last changes fastest.
Arguments:
- model_pert: bfloat16 [64, 64, 1024], P('surveys', 'tx', 'ty'), parts along dimension 0, may hold values from -6 to 6
- station_cells: int32 [8, 4, 512], P(('surveys', 'tx'), 'ty'), parts along dimension 0, may hold values from 0 to 4095, as said below
- station_resid: bfloat16 [8, 4, 48, 512], P(('surveys', 'tx'), 'ty'), parts along dimension 0, may hold values from -6 to 6
- data_weight: int32 [8, 4, 48, 512], P(('surveys', 'tx'), 'ty'), parts along dimension 0, may hold values 0 or 1
- kernels: bfloat16 [48, 32, 9, 9], replicated, may hold values from -0.125 to 0.125
Outputs:
- predicted: float32 [8, 4, 48, 512], P(('surveys', 'tx'), 'ty'), parts along dimension 0
- gradient: float32 [64, 64, 1024], P('surveys', 'tx', 'ty'), parts along dimension 0
There are 2 independent parts, one for each index of `surveys`. A program takes and returns all parts, laid end to end along the dimension named above; an argument that names none is the same for every part. Nothing has to cross between parts.
Inputs may be any that keep to these rules, and one draw needn't show every extreme that they name: `station_cells`: within one tile the 512 station indices are distinct; every tile has a station at its first cell and one at its last cell.
All inputs are finite; a program needn't handle non-finite values. No bound on the sum of `data_weight` on one device may be relied on, other than what follows from the above.
Results may differ from a plain program's by a relative error of at most 0.0003.
Values may be sent and summed in bfloat16 or wider, within the bound.
A program may use at most 64 MiB of HBM per device.

v0:
```python
import functools

import jax
import jax.numpy as jnp
from jax import lax
from jax.experimental import pallas as pl
from jax.experimental.pallas import tpu as pltpu
from jax.sharding import PartitionSpec as P

HALO = 4
TAPS = 9
LANES = 128
EDGE = 16
BF16 = jnp.bfloat16
F32 = jnp.float32
NT = (((1,), (1,)), ((), ()))


def dot_nt(a, b):
    return lax.dot_general(a, b, NT, preferred_element_type=F32)


def dot_nn(a, b):
    return jnp.dot(a, b, preferred_element_type=F32)


def spread_rows(values, station_rows, first, count):
    return jnp.concatenate(
        [jnp.where(station_rows == first + x, values, 0.0).astype(BF16) for x in range(count)],
        axis=0,
    )


def one_hot(ids, count, first=0):
    spot = lax.broadcasted_iota(jnp.int32, (count, ids.shape[1]), 0) + first
    return jnp.where(spot == ids, 1.0, 0.0).astype(BF16)


def exchange_kernel(
    dims,
    cells_ref,
    resid_ref,
    weight_ref,
    model_ref,
    own_model,
    halo_model,
    halo_resid,
    halo_cells,
    edges,
    corners,
    send_resid,
    send_cells,
    send_edges,
    send_sems,
    recv_sems,
):
    tx_count, ty_count, layers, resps, rows, cols = dims
    tx, ty = lax.axis_index("tx"), lax.axis_index("ty")
    has = {-1: tx > 0, 1: tx < tx_count - 1}
    has_col = {-1: ty > 0, 1: ty < ty_count - 1}
    around = [(dx, dy) for dx in (-1, 0, 1) for dy in (-1, 0, 1) if (dx, dy) != (0, 0)]

    def exists(dx, dy):
        ok = None
        for part in ([has[dx]] if dx else []) + ([has_col[dy]] if dy else []):
            ok = part if ok is None else jnp.logical_and(ok, part)
        return ok

    barrier = pltpu.get_barrier_semaphore()
    for dx, dy in around:
        @pl.when(exists(dx, dy))
        def _():
            pl.semaphore_signal(
                barrier,
                inc=1,
                device_id={"tx": tx + dx, "ty": ty + dy},
                device_id_type=pl.DeviceIdType.MESH,
            )

    weighted = resid_ref[...].astype(F32) * weight_ref[...].astype(F32)
    send_resid[...] = weighted.astype(BF16)
    send_cells[...] = jnp.broadcast_to(cells_ref[...], send_cells.shape)

    total = layers * rows
    to = lax.broadcasted_iota(jnp.int32, (total, total), 0)
    frm = lax.broadcasted_iota(jnp.int32, (total, total), 1)
    source = (to % layers) * rows + to // layers
    perm = jnp.where(frm == source, 1.0, 0.0).astype(BF16)
    own_model[...] = dot_nn(perm, model_ref[...]).astype(BF16)

    cells = cells_ref[...]
    row_of, col_of = cells // cols, cells % cols
    spread = spread_rows(weighted, row_of, 0, rows)
    near = lax.broadcasted_iota(jnp.int32, (EDGE, cols), 0)
    lane = lax.broadcasted_iota(jnp.int32, (EDGE, cols), 1)
    for side, first in enumerate((0, cols - EDGE)):
        pick = jnp.where(lane == near + first, 1.0, 0.0).astype(BF16)
        send_edges[side, :, :total] = dot_nt(pick, own_model[...]).astype(BF16)
        send_edges[side, :, total:] = dot_nt(one_hot(col_of, EDGE, first), spread).astype(BF16)

    for side, dx in enumerate((-1, 1)):
        @pl.when(jnp.logical_not(has[dx]))
        def _():
            halo_model[side] = jnp.zeros(halo_model.shape[1:], BF16)
            halo_resid[side] = jnp.zeros(halo_resid.shape[1:], BF16)
            halo_cells[side] = jnp.zeros(halo_cells.shape[1:], jnp.int32)
    for side, dy in enumerate((-1, 1)):
        @pl.when(jnp.logical_not(has_col[dy]))
        def _():
            edges[side] = jnp.zeros(edges.shape[1:], BF16)
    for vert, dx in enumerate((-1, 1)):
        for side, dy in enumerate((-1, 1)):
            @pl.when(jnp.logical_not(exists(dx, dy)))
            def _():
                corners[vert, side] = jnp.zeros(corners.shape[2:], BF16)

    spans = [
        1 + both[-1].astype(jnp.int32) + both[1].astype(jnp.int32) for both in (has, has_col)
    ]
    pl.semaphore_wait(barrier, spans[0] * spans[1] - 1)

    thick = HALO * layers
    wide = corners.shape[-1] - thick

    def copies(dx, dy):
        pairs = []
        if dy == 0:
            mine = 1 if dx == -1 else 0
            start = 0 if dx == -1 else total - thick
            pairs.append((own_model.at[pl.ds(start, thick)], halo_model.at[mine]))
            pairs.append((send_resid, halo_resid.at[mine]))
            pairs.append((send_cells, halo_cells.at[mine]))
        elif dx == 0:
            mine = 1 if dy == -1 else 0
            pairs.append((send_edges.at[1 - mine], edges.at[mine]))
        else:
            vert, side = (1 if dx == -1 else 0), (1 if dy == -1 else 0)
            start = 0 if dx == -1 else total - thick
            start_resid = total if dx == -1 else send_edges.shape[-1] - wide
            src = send_edges.at[1 - side]
            dst = corners.at[vert, side]
            pairs.append((src.at[:, pl.ds(start, thick)], dst.at[:, pl.ds(0, thick)]))
            pairs.append((src.at[:, pl.ds(start_resid, wide)], dst.at[:, pl.ds(thick, wide)]))
        return pairs

    number = {}
    for d in around:
        for c in range(len(copies(*d))):
            number[d, c] = len(number)

    def remote(d, c):
        src, dst = copies(*d)[c]
        return pltpu.make_async_remote_copy(
            src_ref=src,
            dst_ref=dst,
            send_sem=send_sems.at[number[d, c]],
            recv_sem=recv_sems.at[number[d, c]],
            device_id={"tx": tx + d[0], "ty": ty + d[1]},
            device_id_type=pl.DeviceIdType.MESH,
        )

    order = sorted(around, key=lambda d: abs(d[1]))
    for d in order:
        @pl.when(exists(*d))
        def _():
            for c in range(len(copies(*d))):
                remote(d, c).start()
    for d in order:
        @pl.when(exists(*d))
        def _():
            for c in range(len(copies(*d))):
                remote(d, c).wait_send()

        @pl.when(exists(-d[0], -d[1]))
        def _():
            for c in range(len(copies(*d))):
                remote(d, c).wait_recv()


def product_kernel(
    dims,
    cells_ref,
    resid_ref,
    weight_ref,
    own_model,
    halo_model,
    halo_resid,
    halo_cells,
    edges,
    corners,
    forward_ref,
    adjoint_ref,
    predicted_ref,
    gradient_ref,
    padded_f,
    padded_a,
    stack_f,
    stack_a,
    tall_f,
    tall_a,
    toeplitz_f,
    toeplitz_a,
    mixed,
):
    tx_count, ty_count, layers, resps, rows, cols = dims
    tall = rows + 2 * HALO

    def toeplitz(taps_ref, long_ref, out_ref, depth, outs):
        step = TAPS * depth
        gap = (HALO - 1) * step
        size = taps_ref.shape[0]
        long_ref[pl.ds(0, gap), :] = jnp.zeros((gap, outs), BF16)
        long_ref[pl.ds(gap, size), :] = taps_ref[...]
        long_ref[pl.ds(gap + size, gap), :] = jnp.zeros((gap, outs), BF16)
        eye = jnp.where(
            lax.broadcasted_iota(jnp.int32, (outs, outs), 0)
            == lax.broadcasted_iota(jnp.int32, (outs, outs), 1),
            1.0,
            0.0,
        ).astype(BF16)
        width = out_ref.shape[1]
        for a in range(HALO):
            rolled = long_ref[pl.ds(gap - a * step, width), :]
            out_ref[pl.ds(a * outs, outs), :] = dot_nt(eye, rolled).astype(BF16)

    toeplitz(forward_ref, tall_f, toeplitz_f, layers, resps)
    toeplitz(adjoint_ref, tall_a, toeplitz_a, resps, layers)

    weights = weight_ref[...].astype(F32)
    weighted = resid_ref[...].astype(F32) * weights
    cells = cells_ref[...]
    row_of, col_of = cells // cols, cells % cols
    hot = one_hot(col_of, cols)

    total = layers * rows
    thick = HALO * layers
    padded_f[pl.ds(0, thick), LANES : LANES + cols] = halo_model[0]
    padded_f[pl.ds(thick, total), LANES : LANES + cols] = own_model[...]
    padded_f[pl.ds(thick + total, thick), LANES : LANES + cols] = halo_model[1]
    thick_a = HALO * resps
    total_a = resps * rows
    padded_a[pl.ds(thick_a, total_a), LANES : LANES + cols] = dot_nt(
        spread_rows(weighted, row_of, 0, rows), hot
    ).astype(BF16)
    for side in range(2):
        other = halo_cells[side][:1]
        values = halo_resid[side].astype(F32)
        first = rows - HALO if side == 0 else 0
        start = 0 if side == 0 else thick_a + total_a
        padded_a[pl.ds(start, thick_a), LANES : LANES + cols] = dot_nt(
            spread_rows(values, other // cols, first, HALO), one_hot(other % cols, cols)
        ).astype(BF16)
    for side in range(2):
        top, mid, low = corners[0, side], edges[side], corners[1, side]
        line_f = jnp.concatenate([top[:, :thick], mid[:, :total], low[:, :thick]], axis=1)
        wide = corners.shape[-1] - thick
        over = wide - thick_a
        line_a = jnp.concatenate(
            [top[:, thick + over :], mid[:, total:], low[:, thick : thick + thick_a]], axis=1
        )
        for line, padded in ((line_f, padded_f), (line_a, padded_a)):
            blank = jnp.zeros((LANES - EDGE, line.shape[1]), F32)
            line = line.astype(F32)
            if side == 0:
                block = jnp.concatenate([blank, line], axis=0).T
                padded[:, :LANES] = block.astype(BF16)
            else:
                block = jnp.concatenate([line, blank], axis=0).T
                padded[:, LANES + cols :] = block.astype(BF16)

    for padded, stack, depth in ((padded_f, stack_f, layers), (padded_a, stack_a, resps)):
        for x in range(tall):
            block = padded[pl.ds(x * depth, depth), :]
            for q in range(TAPS):
                begin = LANES - HALO + q
                stack[pl.ds((x * TAPS + q) * depth, depth), :] = block[:, begin : begin + cols]

    sampled = None
    for h in range(rows // HALO):
        deep = toeplitz_f.shape[1]
        field = dot_nn(toeplitz_f[...], stack_f[pl.ds(h * HALO * TAPS * layers, deep), :])
        high = field.astype(BF16)
        low = (field - high.astype(F32)).astype(BF16)
        spots = dot_nn(high, hot) + dot_nn(low, hot)
        for a in range(HALO):
            term = jnp.where(row_of == h * HALO + a, spots[a * resps : (a + 1) * resps], 0.0)
            sampled = term if sampled is None else sampled + term
    predicted_ref[...] = sampled * weights

    for h in range(rows // HALO):
        deep = toeplitz_a.shape[1]
        grad = dot_nn(toeplitz_a[...], stack_a[pl.ds(h * HALO * TAPS * resps, deep), :])
        for a in range(HALO):
            for t in range(cols // LANES):
                mixed[t, pl.ds(h * HALO + a, layers, stride=rows), :] = grad[
                    a * layers : (a + 1) * layers, t * LANES : (t + 1) * LANES
                ]
    for t in range(cols // LANES):
        gradient_ref[:, t * LANES : (t + 1) * LANES] = mixed[t]


def shards(tx_count, ty_count, model_pert, station_cells, station_resid, data_weight, kernels):
    layers, rows, cols = model_pert.shape
    resps = kernels.shape[0]
    stations = station_cells.shape[-1]
    dims = (tx_count, ty_count, layers, resps, rows, cols)
    cells, resid, weight = station_cells[0], station_resid[0, 0], data_weight[0, 0]
    model = model_pert.reshape(layers * rows, cols)
    line = (layers + resps) * rows
    thick_a = -(-HALO * resps // LANES) * LANES
    vmem = pl.BlockSpec(memory_space=pltpu.VMEM)
    shape = jax.ShapeDtypeStruct
    copy_count = 2 * 3 + 2 + 4 * 2
    exchanged = pl.pallas_call(
        functools.partial(exchange_kernel, dims),
        out_shape=(
            shape((layers * rows, cols), BF16),
            shape((2, HALO * layers, cols), BF16),
            shape((2, resps, stations), BF16),
            shape((2, 8, stations), jnp.int32),
            shape((2, EDGE, line), BF16),
            shape((2, 2, EDGE, HALO * layers + thick_a), BF16),
        ),
        in_specs=[vmem] * 4,
        out_specs=(vmem,) * 6,
        scratch_shapes=[
            pltpu.VMEM((resps, stations), BF16),
            pltpu.VMEM((8, stations), jnp.int32),
            pltpu.VMEM((2, EDGE, line), BF16),
            pltpu.SemaphoreType.DMA((copy_count,)),
            pltpu.SemaphoreType.DMA((copy_count,)),
        ],
        compiler_params=pltpu.CompilerParams(
            collective_id=0, has_side_effects=True, vmem_limit_bytes=24 * 2**20
        ),
    )(cells, resid, weight, model)

    forward = jnp.transpose(kernels, (2, 3, 1, 0)).reshape(TAPS * TAPS * layers, resps)
    adjoint = jnp.transpose(kernels[:, :, ::-1, ::-1], (2, 3, 0, 1))
    adjoint = adjoint.reshape(TAPS * TAPS * resps, layers)
    tall = rows + 2 * HALO
    reach = TAPS + HALO - 1
    predicted, gradient = pl.pallas_call(
        functools.partial(product_kernel, dims),
        out_shape=(
            shape((resps, stations), F32),
            shape((layers * rows, cols), F32),
        ),
        in_specs=[vmem] * 11,
        out_specs=(vmem,) * 2,
        scratch_shapes=[
            pltpu.VMEM((tall * layers, cols + 2 * LANES), BF16),
            pltpu.VMEM((tall * resps, cols + 2 * LANES), BF16),
            pltpu.VMEM((tall * TAPS * layers, cols), BF16),
            pltpu.VMEM((tall * TAPS * resps, cols), BF16),
            pltpu.VMEM(((TAPS + 2 * (HALO - 1)) * TAPS * layers, resps), BF16),
            pltpu.VMEM(((TAPS + 2 * (HALO - 1)) * TAPS * resps, layers), BF16),
            pltpu.VMEM((HALO * resps, reach * TAPS * layers), BF16),
            pltpu.VMEM((HALO * layers, reach * TAPS * resps), BF16),
            pltpu.VMEM((cols // LANES, layers * rows, LANES), F32),
        ],
        compiler_params=pltpu.CompilerParams(vmem_limit_bytes=40 * 2**20),
    )(cells, resid, weight, *exchanged, forward, adjoint)
    return predicted[None, None], gradient.reshape(layers, rows, cols)


def solution(mesh):
    placed = (
        P("surveys", "tx", "ty"),
        P(("surveys", "tx"), "ty", None),
        P(("surveys", "tx"), "ty", None, None),
        P(("surveys", "tx"), "ty", None, None),
        P(),
    )
    return jax.shard_map(
        functools.partial(shards, mesh.shape["tx"], mesh.shape["ty"]),
        mesh=mesh,
        in_specs=placed,
        out_specs=(P(("surveys", "tx"), "ty", None, None), P("surveys", "tx", "ty")),
        check_vma=False,
    )
```

profile of v0, /device:TPU:0, one launch (start us, length us, event | category | flops | bytes accessed | tf_op | source)
XLA Modules:
  0.0 26.2 jit_solution(18230252529058983294)
XLA Ops:
  0.6 0.0 copy-start.6
  0.6 0.7 %copy-done.6 = s32[1,1,512]{2,1,0:T(1,128)S(1)} copy-done((s32[1,1,512]{2,1,0:T(1,128)S(1)}, s32[1,1,512]{2,1,0:T(1,128)}, u32[]{:S(2)}) %copy-start.6) | copy-done | bytes 2072
  1.3 0.0 copy-start.1
  1.3 0.9 %copy-done.1 = s32[1,1,48,512]{3,2,1,0:T(8,128)S(1)} copy-done((s32[1,1,48,512]{3,2,1,0:T(8,128)S(1)}, s32[1,1,48,512]{3,2,1,0:T(8,128)}, u32[]{:S(2)}) %copy-start.1) | copy-done | bytes 98328
  2.2 0.0 copy-start.3
  2.2 0.9 %copy-done.3 = bf16[32,16,256]{2,1,0:T(8,128)(2,1)S(1)} copy-done((bf16[32,16,256]{2,1,0:T(8,128)(2,1)S(1)}, bf16[32,16,256]{2,1,0:T(8,128)(2,1)}, u32[]{:S(2)}) %copy-start.3) | copy-done | bytes 262168
  3.2 0.0 copy-start.4
  3.2 0.8 %copy-done.4 = bf16[1,1,48,512]{3,2,1,0:T(8,128)(2,1)S(1)} copy-done((bf16[1,1,48,512]{3,2,1,0:T(8,128)(2,1)S(1)}, bf16[1,1,48,512]{3,2,1,0:T(8,128)(2,1)}, u32[]{:S(2)}) %copy-start.4) | copy-done | bytes 49176
  4.0 9.5 %shard_map.68 = (bf16[512,256]{1,0:T(8,128)(2,1)S(1)}, bf16[2,128,256]{2,1,0:T(8,128)(2,1)S(1)}, bf16[2,48,512]{2,1,0:T(8,128)(2,1)S(1)}, s32[2,8,512]{2,1,0:T(8...) custom-call(s32[1,512]{1,0:T(1,128)S(1)} %bitcast.19, bf16[48,512]{1,0:T(8,128)(2,1)S(1)} %bitcast.17, ...), custom_call_target="tpu_custom_call" | custom-call | tf_op jit(solution)/shard_map/pallas_call | solution.py:314
  13.5 1.1 %reverse_bitcast_fusion = bf16[9,9,48,32]{2,3,1,0:T(8,128)(2,1)S(1)} fusion(bf16[48,32,9,9]{0,1,3,2:T(8,128)(2,1)} %param.9), kind=kLoop, calls=%fused_computation | loop fusion | bytes 497664 | tf_op jit(solution)/shard_map/transpose | solution.py:339
  14.6 0.0 copy-start
  14.6 0.0 copy-start.2
  14.6 0.0 copy-start.5
  14.6 1.4 %copy.7 = bf16[9,9,48,32]{3,2,1,0:T(8,128)(2,1)S(1)} copy(bf16[9,9,48,32]{2,3,1,0:T(8,128)(2,1)S(1)} %reverse_bitcast_fusion) | data formatting | bytes 497664 | tf_op jit(solution)/shard_map/transpose | solution.py:339
  16.1 0.0 copy-done
  16.1 0.0 copy-done.2
  16.1 0.0 copy-done.5
  16.1 10.1 %shard_map.69 = (f32[48,512]{1,0:T(8,128)}, f32[512,256]{1,0:T(8,128)}) custom-call(s32[1,512]{1,0:T(1,128)S(1)} %bitcast.20, bf16[48,512]{1,0:T(8,128)(2,1)S(1)} %bitcast.18, s32[48,512]{1,0:T(8,128)S(1)} %bitcast.15, bf16[512,256]{1,0:T(8,128)(2,1)S(1)} %get-tuple-element.10.own_model, bf16[2,128,256]{2,1,0:T(8,128)(2,1)S(1)} %get-tuple-element.11.halo_model, ...), custom_call_target="tpu_custom_call" | custom-call | tf_op jit(solution)/shard_map/pallas_call | solution.py:343
Async XLA Ops:
  0.6 0.7 %copy-start.6 = (s32[1,1,512]{2,1,0:T(1,128)S(1)}, s32[1,1,512]{2,1,0:T(1,128)}, u32[]{:S(2)}) copy-start(s32[1,1,512]{2,1,0:T(1,128)} %param.6) | copy-start | bytes 6148
  1.3 0.9 %copy-start.1 = (s32[1,1,48,512]{3,2,1,0:T(8,128)S(1)}, s32[1,1,48,512]{3,2,1,0:T(8,128)}, u32[]{:S(2)}) copy-start(s32[1,1,48,512]{3,2,1,0:T(8,128)} %param.8) | copy-start | bytes 294916
  2.2 0.9 %copy-start.3 = (bf16[32,16,256]{2,1,0:T(8,128)(2,1)S(1)}, bf16[32,16,256]{2,1,0:T(8,128)(2,1)}, u32[]{:S(2)}) copy-start(bf16[32,16,256]{2,1,0:T(8,128)(2,1)} %param.5) | copy-start | bytes 786436
  3.2 0.8 %copy-start.4 = (bf16[1,1,48,512]{3,2,1,0:T(8,128)(2,1)S(1)}, bf16[1,1,48,512]{3,2,1,0:T(8,128)(2,1)}, u32[]{:S(2)}) copy-start(bf16[1,1,48,512]{3,2,1,0:T(8,128)(2,1)} %param.7) | copy-start | bytes 147460
  14.6 1.5 %copy-start = (bf16[48,32,9,9]{0,1,3,2:T(8,128)(2,1)S(1)}, bf16[48,32,9,9]{0,1,3,2:T(8,128)(2,1)}, u32[]{:S(2)}) copy-start(bf16[48,32,9,9]{0,1,3,2:T(8,128)(2,1)} %param.9) | copy-start | bytes 746500
  14.6 1.5 %copy-start.2 = (s32[1,1,48,512]{3,2,1,0:T(8,128)S(1)}, s32[1,1,48,512]{3,2,1,0:T(8,128)}, u32[]{:S(2)}) copy-start(s32[1,1,48,512]{3,2,1,0:T(8,128)} %param.8) | copy-start | bytes 294916
  14.6 1.4 %copy-start.5 = (bf16[1,1,48,512]{3,2,1,0:T(8,128)(2,1)S(1)}, bf16[1,1,48,512]{3,2,1,0:T(8,128)(2,1)}, u32[]{:S(2)}) copy-start(bf16[1,1,48,512]{3,2,1,0:T(8,128)(2,1)} %param.7) | copy-start | bytes 147460
where the time goes:
time: 26.5 us; the launch traced here: 26.2 us
  Pallas kernels  19.6 us (74%)
  local copies, waits for them, and re-layouts  5.88 us (22%)
  between operations  0.71 us (3%)
    pallas_call x1, Pallas kernels, shards(): pl.pallas_call(functools.partial(product_kernel, dims), out_shape=(shape(...  10.1 us
    pallas_call x1, Pallas kernels, shards(): pl.pallas_call(functools.partial(exchange_kernel, dims), out_shape=(shape...  9.5 us
    unnamed x14, local copies, waits for them, and re-layouts  3.33 us
    transpose x2, local copies, waits for them, and re-layouts, shards(): adjoint = jnp.transpose(kernels[:, :, ::-1, ::-1], (2, 3, 0, 1))  2.54 us

commit v1 on v0

--- a/solution.py
+++ b/solution.py
@@ -1,4 +1,5 @@
 import functools
+import math
 
 import jax
 import jax.numpy as jnp
@@ -36,21 +37,41 @@
     return jnp.where(spot == ids, 1.0, 0.0).astype(BF16)
 
 
+def round_up(size):
+    return -(-size // LANES) * LANES
+
+
+def offsets(depth):
+    return round_up((HALO - 1) * TAPS * depth)
+
+
 def exchange_kernel(
     dims,
-    cells_ref,
-    resid_ref,
+    cells_hbm,
+    resid_hbm,
+    weight_hbm,
+    model_hbm,
+    taps_hbm,
     weight_ref,
-    model_ref,
+    send_cells,
+    own_resid,
+    toeplitz_f,
+    toeplitz_a,
     own_model,
     halo_model,
     halo_resid,
     halo_cells,
     edges,
     corners,
+    cells_ref,
+    resid_ref,
+    model_ref,
+    taps_ref,
+    base_f,
+    base_a,
     send_resid,
-    send_cells,
     send_edges,
+    load_sems,
     send_sems,
     recv_sems,
 ):
@@ -66,6 +87,20 @@
             ok = part if ok is None else jnp.logical_and(ok, part)
         return ok
 
+    loads = [
+        pltpu.make_async_copy(src, dst, load_sems.at[n])
+        for n, (src, dst) in enumerate(
+            (
+                (cells_hbm, cells_ref),
+                (resid_hbm, resid_ref),
+                (weight_hbm, weight_ref),
+                (model_hbm, model_ref),
+                (taps_hbm, taps_ref),
+            )
+        )
+    ]
+    for load in loads:
+        load.start()
     barrier = pltpu.get_barrier_semaphore()
     for dx, dy in around:
         @pl.when(exists(dx, dy))
@@ -77,27 +112,6 @@
                 device_id_type=pl.DeviceIdType.MESH,
             )
 
-    weighted = resid_ref[...].astype(F32) * weight_ref[...].astype(F32)
-    send_resid[...] = weighted.astype(BF16)
-    send_cells[...] = jnp.broadcast_to(cells_ref[...], send_cells.shape)
-
-    total = layers * rows
-    to = lax.broadcasted_iota(jnp.int32, (total, total), 0)
-    frm = lax.broadcasted_iota(jnp.int32, (total, total), 1)
-    source = (to % layers) * rows + to // layers
-    perm = jnp.where(frm == source, 1.0, 0.0).astype(BF16)
-    own_model[...] = dot_nn(perm, model_ref[...]).astype(BF16)
-
-    cells = cells_ref[...]
-    row_of, col_of = cells // cols, cells % cols
-    spread = spread_rows(weighted, row_of, 0, rows)
-    near = lax.broadcasted_iota(jnp.int32, (EDGE, cols), 0)
-    lane = lax.broadcasted_iota(jnp.int32, (EDGE, cols), 1)
-    for side, first in enumerate((0, cols - EDGE)):
-        pick = jnp.where(lane == near + first, 1.0, 0.0).astype(BF16)
-        send_edges[side, :, :total] = dot_nt(pick, own_model[...]).astype(BF16)
-        send_edges[side, :, total:] = dot_nt(one_hot(col_of, EDGE, first), spread).astype(BF16)
-
     for side, dx in enumerate((-1, 1)):
         @pl.when(jnp.logical_not(has[dx]))
         def _():
@@ -113,6 +127,20 @@
             @pl.when(jnp.logical_not(exists(dx, dy)))
             def _():
                 corners[vert, side] = jnp.zeros(corners.shape[2:], BF16)
+
+    for load in loads[:3]:
+        load.wait()
+    weighted = resid_ref[...].astype(F32) * weight_ref[...].astype(F32)
+    send_resid[...] = weighted.astype(BF16)
+    send_cells[...] = jnp.broadcast_to(cells_ref[...], send_cells.shape)
+
+    total = layers * rows
+    loads[3].wait()
+    to = lax.broadcasted_iota(jnp.int32, (total, total), 0)
+    frm = lax.broadcasted_iota(jnp.int32, (total, total), 1)
+    source = (to % layers) * rows + to // layers
+    perm = jnp.where(frm == source, 1.0, 0.0).astype(BF16)
+    own_model[...] = dot_nn(perm, model_ref[...]).astype(BF16)
 
     spans = [
         1 + both[-1].astype(jnp.int32) + both[1].astype(jnp.int32) for both in (has, has_col)
@@ -160,15 +188,65 @@
         )
 
     order = sorted(around, key=lambda d: abs(d[1]))
+
+    def start(d):
+        @pl.when(exists(*d))
+        def _():
+            for c in range(len(copies(*d))):
+                remote(d, c).start()
+
+    for d in order[:2]:
+        start(d)
+
+    cells = cells_ref[...]
+    row_of, col_of = cells // cols, cells % cols
+    spread = spread_rows(weighted, row_of, 0, rows)
+    near = lax.broadcasted_iota(jnp.int32, (EDGE, cols), 0)
+    lane = lax.broadcasted_iota(jnp.int32, (EDGE, cols), 1)
+    for side, first in enumerate((0, cols - EDGE)):
+        pick = jnp.where(lane == near + first, 1.0, 0.0).astype(BF16)
+        send_edges[side, :, :total] = dot_nt(pick, own_model[...]).astype(BF16)
+        send_edges[side, :, total:] = dot_nt(one_hot(col_of, EDGE, first), spread).astype(BF16)
+
+    for d in order[2:]:
+        start(d)
+
+    own_resid[...] = dot_nt(spread, one_hot(col_of, cols)).astype(BF16)
+
+    loads[4].wait()
+    offset_f, offset_a = offsets(layers), offsets(resps)
+    eye = jnp.where(
+        lax.broadcasted_iota(jnp.int32, (resps, resps), 0)
+        == lax.broadcasted_iota(jnp.int32, (resps, resps), 1),
+        1.0,
+        0.0,
+    ).astype(BF16)
+    base_f[...] = jnp.zeros_like(base_f)
+    size_f = TAPS * TAPS * layers
+    base_f[:, offset_f : offset_f + size_f] = dot_nt(eye, taps_ref[...]).astype(BF16)
+    base_a[...] = jnp.zeros_like(base_a)
+    group = LANES // math.gcd(LANES, resps)
+    for lead in range(0, TAPS * TAPS, group):
+        blocks = [
+            taps_ref[pl.ds((TAPS * TAPS - 1 - m) * layers, layers), :]
+            for m in range(lead, min(lead + group, TAPS * TAPS))
+        ]
+        begin = offset_a + lead * resps
+        base_a[:, begin : begin + len(blocks) * resps] = jnp.concatenate(blocks, axis=1)
+    for base, out, offset, depth in (
+        (base_f, toeplitz_f, offset_f, layers),
+        (base_a, toeplitz_a, offset_a, resps),
+    ):
+        height, width = base.shape[0], out.shape[1]
+        whole = base[...]
+        for a in range(HALO):
+            begin = offset - a * TAPS * depth
+            out[pl.ds(a * height, height), :] = whole[:, begin : begin + width]
+
     for d in order:
         @pl.when(exists(*d))
         def _():
             for c in range(len(copies(*d))):
-                remote(d, c).start()
-    for d in order:
-        @pl.when(exists(*d))
-        def _():
-            for c in range(len(copies(*d))):
                 remote(d, c).wait_send()
 
         @pl.when(exists(-d[0], -d[1]))
@@ -179,56 +257,30 @@
 
 def product_kernel(
     dims,
+    weight_ref,
     cells_ref,
-    resid_ref,
-    weight_ref,
+    own_resid,
+    toeplitz_f,
+    toeplitz_a,
     own_model,
     halo_model,
     halo_resid,
     halo_cells,
     edges,
     corners,
-    forward_ref,
-    adjoint_ref,
     predicted_ref,
     gradient_ref,
     padded_f,
     padded_a,
     stack_f,
     stack_a,
-    tall_f,
-    tall_a,
-    toeplitz_f,
-    toeplitz_a,
     mixed,
 ):
     tx_count, ty_count, layers, resps, rows, cols = dims
     tall = rows + 2 * HALO
 
-    def toeplitz(taps_ref, long_ref, out_ref, depth, outs):
-        step = TAPS * depth
-        gap = (HALO - 1) * step
-        size = taps_ref.shape[0]
-        long_ref[pl.ds(0, gap), :] = jnp.zeros((gap, outs), BF16)
-        long_ref[pl.ds(gap, size), :] = taps_ref[...]
-        long_ref[pl.ds(gap + size, gap), :] = jnp.zeros((gap, outs), BF16)
-        eye = jnp.where(
-            lax.broadcasted_iota(jnp.int32, (outs, outs), 0)
-            == lax.broadcasted_iota(jnp.int32, (outs, outs), 1),
-            1.0,
-            0.0,
-        ).astype(BF16)
-        width = out_ref.shape[1]
-        for a in range(HALO):
-            rolled = long_ref[pl.ds(gap - a * step, width), :]
-            out_ref[pl.ds(a * outs, outs), :] = dot_nt(eye, rolled).astype(BF16)
-
-    toeplitz(forward_ref, tall_f, toeplitz_f, layers, resps)
-    toeplitz(adjoint_ref, tall_a, toeplitz_a, resps, layers)
-
     weights = weight_ref[...].astype(F32)
-    weighted = resid_ref[...].astype(F32) * weights
-    cells = cells_ref[...]
+    cells = cells_ref[:1, :]
     row_of, col_of = cells // cols, cells % cols
     hot = one_hot(col_of, cols)
 
@@ -239,9 +291,7 @@
     padded_f[pl.ds(thick + total, thick), LANES : LANES + cols] = halo_model[1]
     thick_a = HALO * resps
     total_a = resps * rows
-    padded_a[pl.ds(thick_a, total_a), LANES : LANES + cols] = dot_nt(
-        spread_rows(weighted, row_of, 0, rows), hot
-    ).astype(BF16)
+    padded_a[pl.ds(thick_a, total_a), LANES : LANES + cols] = own_resid[...]
     for side in range(2):
         other = halo_cells[side][:1]
         values = halo_resid[side].astype(F32)
@@ -311,9 +361,18 @@
     vmem = pl.BlockSpec(memory_space=pltpu.VMEM)
     shape = jax.ShapeDtypeStruct
     copy_count = 2 * 3 + 2 + 4 * 2
+    hbm = pl.BlockSpec(memory_space=pltpu.HBM)
+    reach = TAPS + HALO - 1
+    wide_f, wide_a = reach * TAPS * layers, reach * TAPS * resps
+    forward = jnp.transpose(kernels, (2, 3, 1, 0)).reshape(TAPS * TAPS * layers, resps)
     exchanged = pl.pallas_call(
         functools.partial(exchange_kernel, dims),
         out_shape=(
+            shape((resps, stations), jnp.int32),
+            shape((8, stations), jnp.int32),
+            shape((resps * rows, cols), BF16),
+            shape((HALO * resps, wide_f), BF16),
+            shape((HALO * layers, wide_a), BF16),
             shape((layers * rows, cols), BF16),
             shape((2, HALO * layers, cols), BF16),
             shape((2, resps, stations), BF16),
@@ -321,25 +380,27 @@
             shape((2, EDGE, line), BF16),
             shape((2, 2, EDGE, HALO * layers + thick_a), BF16),
         ),
-        in_specs=[vmem] * 4,
-        out_specs=(vmem,) * 6,
+        in_specs=[hbm] * 5,
+        out_specs=(vmem,) * 11,
         scratch_shapes=[
+            pltpu.VMEM((1, stations), jnp.int32),
             pltpu.VMEM((resps, stations), BF16),
-            pltpu.VMEM((8, stations), jnp.int32),
+            pltpu.VMEM((layers * rows, cols), BF16),
+            pltpu.VMEM((TAPS * TAPS * layers, resps), BF16),
+            pltpu.VMEM((resps, round_up(offsets(layers) + wide_f)), BF16),
+            pltpu.VMEM((layers, round_up(offsets(resps) + wide_a)), BF16),
+            pltpu.VMEM((resps, stations), BF16),
             pltpu.VMEM((2, EDGE, line), BF16),
+            pltpu.SemaphoreType.DMA((5,)),
             pltpu.SemaphoreType.DMA((copy_count,)),
             pltpu.SemaphoreType.DMA((copy_count,)),
         ],
         compiler_params=pltpu.CompilerParams(
             collective_id=0, has_side_effects=True, vmem_limit_bytes=24 * 2**20
         ),
-    )(cells, resid, weight, model)
-
-    forward = jnp.transpose(kernels, (2, 3, 1, 0)).reshape(TAPS * TAPS * layers, resps)
-    adjoint = jnp.transpose(kernels[:, :, ::-1, ::-1], (2, 3, 0, 1))
-    adjoint = adjoint.reshape(TAPS * TAPS * resps, layers)
+    )(cells, resid, weight, model, forward)
+
     tall = rows + 2 * HALO
-    reach = TAPS + HALO - 1
     predicted, gradient = pl.pallas_call(
         functools.partial(product_kernel, dims),
         out_shape=(
@@ -353,14 +414,10 @@
             pltpu.VMEM((tall * resps, cols + 2 * LANES), BF16),
             pltpu.VMEM((tall * TAPS * layers, cols), BF16),
             pltpu.VMEM((tall * TAPS * resps, cols), BF16),
-            pltpu.VMEM(((TAPS + 2 * (HALO - 1)) * TAPS * layers, resps), BF16),
-            pltpu.VMEM(((TAPS + 2 * (HALO - 1)) * TAPS * resps, layers), BF16),
-            pltpu.VMEM((HALO * resps, reach * TAPS * layers), BF16),
-            pltpu.VMEM((HALO * layers, reach * TAPS * resps), BF16),
             pltpu.VMEM((cols // LANES, layers * rows, LANES), F32),
         ],
-        compiler_params=pltpu.CompilerParams(vmem_limit_bytes=40 * 2**20),
-    )(cells, resid, weight, *exchanged, forward, adjoint)
+        compiler_params=pltpu.CompilerParams(vmem_limit_bytes=32 * 2**20),
+    )(*exchanged)
     return predicted[None, None], gradient.reshape(layers, rows, cols)
 
 

time: 26.5 us -> 22.4 us (0.85)
  Pallas kernels: 19.6 us -> 17.1 us
  local copies, waits for them, and re-layouts: 5.88 us -> 4.4 us
    pallas_call x1, Pallas kernels: 10.1 us -> 7.11 us  [shards(): pl.pallas_call(functools.partial(product_kernel, dims), out_shape=(shape(...]
    transpose x2 -> x0, local copies, waits for them, and re-layouts: 2.54 us -> none  [shards(): adjoint = jnp.transpose(kernels[:, :, ::-1, ::-1], (2, 3, 0, 1))]
    unnamed x14 -> x10, local copies, waits for them, and re-layouts: 3.33 us -> 4.4 us
    pallas_call x1, Pallas kernels: 9.5 us -> 9.96 us  [shards(): pl.pallas_call(functools.partial(exchange_kernel, dims), out_shape=(shape...]
where the time goes in v1:
time: 22.4 us; the launch traced here: 22.1 us
  Pallas kernels  17.1 us (76%)
  local copies, waits for them, and re-layouts  4.4 us (20%)
  between operations  0.65 us (3%)
    pallas_call x1, Pallas kernels, shards(): pl.pallas_call(functools.partial(exchange_kernel, dims), out_shape=(shape...  9.96 us
    pallas_call x1, Pallas kernels, shards(): pl.pallas_call(functools.partial(product_kernel, dims), out_shape=(shape(...  7.11 us
    unnamed x10, local copies, waits for them, and re-layouts  4.4 us

profile of v1, /device:TPU:0, one launch (start us, length us, event | category | flops | bytes accessed | tf_op | source)
XLA Modules:
  0.0 22.1 jit_solution(14044260514974259547)
XLA Ops:
  0.6 0.0 copy-start
  0.6 1.1 %copy-done = bf16[48,32,9,9]{0,1,3,2:T(8,128)(2,1)S(1)} copy-done((bf16[48,32,9,9]{0,1,3,2:T(8,128)(2,1)S(1)}, bf16[48,32,9,9]{0,1,3,2:T(8,128)(2,1)}, u32[]{:S(2)}) %copy-start) | copy-done | bytes 248856
  1.7 0.0 copy-start.1
  1.7 0.9 %copy-done.1 = bf16[32,16,256]{2,1,0:T(8,128)(2,1)S(1)} copy-done((bf16[32,16,256]{2,1,0:T(8,128)(2,1)S(1)}, bf16[32,16,256]{2,1,0:T(8,128)(2,1)}, u32[]{:S(2)}) %copy-start.1) | copy-done | bytes 262168
  2.7 0.0 copy-start.2
  2.7 0.9 %copy-done.2 = s32[1,1,48,512]{3,2,1,0:T(8,128)S(1)} copy-done((s32[1,1,48,512]{3,2,1,0:T(8,128)S(1)}, s32[1,1,48,512]{3,2,1,0:T(8,128)}, u32[]{:S(2)}) %copy-start.2) | copy-done | bytes 98328
  3.6 0.0 copy-start.3
  3.6 0.8 %copy-done.3 = bf16[1,1,48,512]{3,2,1,0:T(8,128)(2,1)S(1)} copy-done((bf16[1,1,48,512]{3,2,1,0:T(8,128)(2,1)S(1)}, bf16[1,1,48,512]{3,2,1,0:T(8,128)(2,1)}, u32[]{:S(2)}) %copy-start.3) | copy-done | bytes 49176
  4.4 0.0 copy-start.4
  4.4 0.7 %copy-done.4 = s32[1,1,512]{2,1,0:T(1,128)S(1)} copy-done((s32[1,1,512]{2,1,0:T(1,128)S(1)}, s32[1,1,512]{2,1,0:T(1,128)}, u32[]{:S(2)}) %copy-start.4) | copy-done | bytes 2072
  5.0 10.0 %shard_map.68 = (s32[48,512]{1,0:T(8,128)S(1)}, s32[8,512]{1,0:T(8,128)S(1)}, bf16[768,256]{1,0:T(8,128)(2,1)S(1)}, bf16[192,3456]{1,0:T(8,128)(2,1)S(1)}, bf16[...) custom-call(s32[1,512]{1,0:T(1,128)S(1)} %bitcast.13, ...), custom_call_target="tpu_custom_call" | custom-call | tf_op jit(solution)/shard_map/pallas_call | solution.py:368
  15.0 7.1 %shard_map.69 = (f32[48,512]{1,0:T(8,128)}, f32[512,256]{1,0:T(8,128)}) custom-call(s32[48,512]{1,0:T(8,128)S(1)} %get-tuple-element.15.weight_ref, s32[8,512]{1,0:T(8,128)S(1)} %get-tuple-element.16.cells_ref, bf16[768,256]{1,0:T(8,128)(2,1)S(1)} %get-tuple-element.17.own_resid, bf16[192,3456]{1,0:T(8,128)(2,1)S(1)} %get-tuple-element.18.toeplitz_f, ...), custom_call_target="tpu_custom_call" | custom-call | tf_op jit(solution)/shard_map/pallas_call | solution.py:404
Async XLA Ops:
  0.6 1.1 %copy-start = (bf16[48,32,9,9]{0,1,3,2:T(8,128)(2,1)S(1)}, bf16[48,32,9,9]{0,1,3,2:T(8,128)(2,1)}, u32[]{:S(2)}) copy-start(bf16[48,32,9,9]{0,1,3,2:T(8,128)(2,1)} %param.9) | copy-start | bytes 746500
  1.7 0.9 %copy-start.1 = (bf16[32,16,256]{2,1,0:T(8,128)(2,1)S(1)}, bf16[32,16,256]{2,1,0:T(8,128)(2,1)}, u32[]{:S(2)}) copy-start(bf16[32,16,256]{2,1,0:T(8,128)(2,1)} %param.5) | copy-start | bytes 786436
  2.7 0.9 %copy-start.2 = (s32[1,1,48,512]{3,2,1,0:T(8,128)S(1)}, s32[1,1,48,512]{3,2,1,0:T(8,128)}, u32[]{:S(2)}) copy-start(s32[1,1,48,512]{3,2,1,0:T(8,128)} %param.8) | copy-start | bytes 294916
  3.6 0.8 %copy-start.3 = (bf16[1,1,48,512]{3,2,1,0:T(8,128)(2,1)S(1)}, bf16[1,1,48,512]{3,2,1,0:T(8,128)(2,1)}, u32[]{:S(2)}) copy-start(bf16[1,1,48,512]{3,2,1,0:T(8,128)(2,1)} %param.7) | copy-start | bytes 147460
  4.4 0.7 %copy-start.4 = (s32[1,1,512]{2,1,0:T(1,128)S(1)}, s32[1,1,512]{2,1,0:T(1,128)}, u32[]{:S(2)}) copy-start(s32[1,1,512]{2,1,0:T(1,128)} %param.6) | copy-start | bytes 6148

commit v2 on v1

--- a/solution.py
+++ b/solution.py
@@ -349,6 +349,12 @@
         gradient_ref[:, t * LANES : (t + 1) * LANES] = mixed[t]
 
 
+def fused_kernel(dims, *refs):
+    arrays, results, scratch = refs[:5], refs[5:7], refs[7:]
+    exchange_kernel(dims, *arrays, *scratch[:22])
+    product_kernel(dims, *scratch[:11], *results, *scratch[22:])
+
+
 def shards(tx_count, ty_count, model_pert, station_cells, station_resid, data_weight, kernels):
     layers, rows, cols = model_pert.shape
     resps = kernels.shape[0]
@@ -365,24 +371,27 @@
     reach = TAPS + HALO - 1
     wide_f, wide_a = reach * TAPS * layers, reach * TAPS * resps
     forward = jnp.transpose(kernels, (2, 3, 1, 0)).reshape(TAPS * TAPS * layers, resps)
-    exchanged = pl.pallas_call(
-        functools.partial(exchange_kernel, dims),
+    tall = rows + 2 * HALO
+    predicted, gradient = pl.pallas_call(
+        functools.partial(fused_kernel, dims),
         out_shape=(
-            shape((resps, stations), jnp.int32),
-            shape((8, stations), jnp.int32),
-            shape((resps * rows, cols), BF16),
-            shape((HALO * resps, wide_f), BF16),
-            shape((HALO * layers, wide_a), BF16),
-            shape((layers * rows, cols), BF16),
-            shape((2, HALO * layers, cols), BF16),
-            shape((2, resps, stations), BF16),
-            shape((2, 8, stations), jnp.int32),
-            shape((2, EDGE, line), BF16),
-            shape((2, 2, EDGE, HALO * layers + thick_a), BF16),
+            shape((resps, stations), F32),
+            shape((layers * rows, cols), F32),
         ),
         in_specs=[hbm] * 5,
-        out_specs=(vmem,) * 11,
+        out_specs=(vmem,) * 2,
         scratch_shapes=[
+            pltpu.VMEM((resps, stations), jnp.int32),
+            pltpu.VMEM((8, stations), jnp.int32),
+            pltpu.VMEM((resps * rows, cols), BF16),
+            pltpu.VMEM((HALO * resps, wide_f), BF16),
+            pltpu.VMEM((HALO * layers, wide_a), BF16),
+            pltpu.VMEM((layers * rows, cols), BF16),
+            pltpu.VMEM((2, HALO * layers, cols), BF16),
+            pltpu.VMEM((2, resps, stations), BF16),
+            pltpu.VMEM((2, 8, stations), jnp.int32),
+            pltpu.VMEM((2, EDGE, line), BF16),
+            pltpu.VMEM((2, 2, EDGE, HALO * layers + thick_a), BF16),
             pltpu.VMEM((1, stations), jnp.int32),
             pltpu.VMEM((resps, stations), BF16),
             pltpu.VMEM((layers * rows, cols), BF16),
@@ -394,30 +403,16 @@
             pltpu.SemaphoreType.DMA((5,)),
             pltpu.SemaphoreType.DMA((copy_count,)),
             pltpu.SemaphoreType.DMA((copy_count,)),
-        ],
-        compiler_params=pltpu.CompilerParams(
-            collective_id=0, has_side_effects=True, vmem_limit_bytes=24 * 2**20
-        ),
-    )(cells, resid, weight, model, forward)
-
-    tall = rows + 2 * HALO
-    predicted, gradient = pl.pallas_call(
-        functools.partial(product_kernel, dims),
-        out_shape=(
-            shape((resps, stations), F32),
-            shape((layers * rows, cols), F32),
-        ),
-        in_specs=[vmem] * 11,
-        out_specs=(vmem,) * 2,
-        scratch_shapes=[
             pltpu.VMEM((tall * layers, cols + 2 * LANES), BF16),
             pltpu.VMEM((tall * resps, cols + 2 * LANES), BF16),
             pltpu.VMEM((tall * TAPS * layers, cols), BF16),
             pltpu.VMEM((tall * TAPS * resps, cols), BF16),
             pltpu.VMEM((cols // LANES, layers * rows, LANES), F32),
         ],
-        compiler_params=pltpu.CompilerParams(vmem_limit_bytes=32 * 2**20),
-    )(*exchanged)
+        compiler_params=pltpu.CompilerParams(
+            collective_id=0, has_side_effects=True, vmem_limit_bytes=60 * 2**20
+        ),
+    )(cells, resid, weight, model, forward)
     return predicted[None, None], gradient.reshape(layers, rows, cols)
 
 

time: 22.4 us -> 21 us (0.938)
  local copies, waits for them, and re-layouts: 4.4 us -> 3.41 us
  Pallas kernels: 17.1 us -> 16.7 us
    unnamed x10 -> x2, local copies, waits for them, and re-layouts: 4.4 us -> 3.41 us
    pallas_call x2 -> x1, Pallas kernels: 17.1 us -> 16.7 us  [shards(): pl.pallas_call(functools.partial(fused_kernel, dims), out_shape=(shape((r...]
where the time goes in v2:
time: 21 us; the launch traced here: 20.8 us
  Pallas kernels  16.7 us (80%)
  local copies, waits for them, and re-layouts  3.41 us (16%)
  between operations  0.64 us (3%)
    pallas_call x1, Pallas kernels, shards(): pl.pallas_call(functools.partial(fused_kernel, dims), out_shape=(shape((r...  16.7 us
    unnamed x2, local copies, waits for them, and re-layouts  3.41 us

profile of v2, /device:TPU:0, one launch (start us, length us, event | category | flops | bytes accessed | tf_op | source)
XLA Modules:
  0.0 20.8 jit_solution(11578706665585288256)
XLA Ops:
  0.6 16.7 %shard_map.68 = (f32[48,512]{1,0:T(8,128)}, f32[512,256]{1,0:T(8,128)}) custom-call(s32[1,512]{1,0:T(1,128)} %bitcast.15, bf16[48,512]{1,0:T(8,128)(2,1)} %bitcast.14, s32[48,512]{1,0:T(8,128)} %bitcast.12, bf16[512,256]{1,0:T(8,128)(2,1)} %bitcast.11, bf16[2592,48]{1,0:T(8,128)(2,1)} %bitcast.9), custom_call_target="tpu_custom_call" | custom-call | tf_op jit(solution)/shard_map/pallas_call | solution.py:375
  17.4 1.5 %copy.9 = f32[1,1,48,512]{3,2,1,0:T(8,128)} copy(f32[1,1,48,512]{3,2,1,0:T(8,128)} %bitcast.13) | data formatting | bytes 196608
  18.9 1.9 %copy.10 = f32[32,16,256]{2,1,0:T(8,128)} copy(f32[32,16,256]{2,1,0:T(8,128)} %bitcast.10) | data formatting | bytes 1048576

commit v3 on v2

--- a/solution.py
+++ b/solution.py
@@ -243,20 +243,29 @@
             begin = offset - a * TAPS * depth
             out[pl.ds(a * height, height), :] = whole[:, begin : begin + width]
 
-    for d in order:
-        @pl.when(exists(*d))
-        def _():
-            for c in range(len(copies(*d))):
-                remote(d, c).wait_send()
-
-        @pl.when(exists(-d[0], -d[1]))
-        def _():
-            for c in range(len(copies(*d))):
-                remote(d, c).wait_recv()
+    def arrive(chosen):
+        for d in chosen:
+            @pl.when(exists(-d[0], -d[1]))
+            def _():
+                for c in range(len(copies(*d))):
+                    remote(d, c).wait_recv()
+
+    def finish():
+        for d in order:
+            @pl.when(exists(*d))
+            def _():
+                for c in range(len(copies(*d))):
+                    remote(d, c).wait_send()
+
+    beside = [d for d in order if d[0] == 0]
+    across = [d for d in order if d[0] != 0]
+    return functools.partial(arrive, beside), functools.partial(arrive, across), finish
 
 
 def product_kernel(
     dims,
+    arrive_beside,
+    arrive_across,
     weight_ref,
     cells_ref,
     own_resid,
@@ -286,73 +295,89 @@
 
     total = layers * rows
     thick = HALO * layers
-    padded_f[pl.ds(0, thick), LANES : LANES + cols] = halo_model[0]
-    padded_f[pl.ds(thick, total), LANES : LANES + cols] = own_model[...]
-    padded_f[pl.ds(thick + total, thick), LANES : LANES + cols] = halo_model[1]
     thick_a = HALO * resps
     total_a = resps * rows
-    padded_a[pl.ds(thick_a, total_a), LANES : LANES + cols] = own_resid[...]
+    centre = slice(LANES, LANES + cols)
+    wide = corners.shape[-1] - thick
+    over = wide - thick_a
+
+    def put_columns(line, padded, start, side):
+        blank = jnp.zeros((LANES - EDGE, line.shape[1]), F32)
+        line = line.astype(F32)
+        if side == 0:
+            block = jnp.concatenate([blank, line], axis=0).T
+            padded[pl.ds(start, block.shape[0]), :LANES] = block.astype(BF16)
+        else:
+            block = jnp.concatenate([line, blank], axis=0).T
+            padded[pl.ds(start, block.shape[0]), LANES + cols :] = block.astype(BF16)
+
+    def shift(rows_of):
+        for padded, stack, depth in ((padded_f, stack_f, layers), (padded_a, stack_a, resps)):
+            for x in rows_of:
+                block = padded[pl.ds(x * depth, depth), :]
+                for q in range(TAPS):
+                    begin = LANES - HALO + q
+                    stack[pl.ds((x * TAPS + q) * depth, depth), :] = block[:, begin : begin + cols]
+
+    def products(groups, sampled):
+        for h in groups:
+            deep = toeplitz_f.shape[1]
+            field = dot_nn(toeplitz_f[...], stack_f[pl.ds(h * HALO * TAPS * layers, deep), :])
+            high = field.astype(BF16)
+            low = (field - high.astype(F32)).astype(BF16)
+            spots = dot_nn(high, hot) + dot_nn(low, hot)
+            for a in range(HALO):
+                term = jnp.where(
+                    row_of == h * HALO + a, spots[a * resps : (a + 1) * resps], 0.0
+                )
+                sampled = term if sampled is None else sampled + term
+            deep = toeplitz_a.shape[1]
+            grad = dot_nn(toeplitz_a[...], stack_a[pl.ds(h * HALO * TAPS * resps, deep), :])
+            for a in range(HALO):
+                for t in range(cols // LANES):
+                    mixed[t, pl.ds(h * HALO + a, layers, stride=rows), :] = grad[
+                        a * layers : (a + 1) * layers, t * LANES : (t + 1) * LANES
+                    ]
+        return sampled
+
+    padded_f[pl.ds(thick, total), centre] = own_model[...]
+    padded_a[pl.ds(thick_a, total_a), centre] = own_resid[...]
+    arrive_beside()
     for side in range(2):
-        other = halo_cells[side][:1]
-        values = halo_resid[side].astype(F32)
-        first = rows - HALO if side == 0 else 0
-        start = 0 if side == 0 else thick_a + total_a
-        padded_a[pl.ds(start, thick_a), LANES : LANES + cols] = dot_nt(
+        put_columns(edges[side][:, :total], padded_f, thick, side)
+        put_columns(edges[side][:, total:], padded_a, thick_a, side)
+    shift(range(HALO, HALO + rows))
+    last = rows // HALO - 1
+    sampled = products(range(1, last), None)
+
+    arrive_across()
+    for vert in range(2):
+        start_f = 0 if vert == 0 else thick + total
+        start_a = 0 if vert == 0 else thick_a + total_a
+        padded_f[pl.ds(start_f, thick), centre] = halo_model[vert]
+        other = halo_cells[vert][:1]
+        values = halo_resid[vert].astype(F32)
+        first = rows - HALO if vert == 0 else 0
+        padded_a[pl.ds(start_a, thick_a), centre] = dot_nt(
             spread_rows(values, other // cols, first, HALO), one_hot(other % cols, cols)
         ).astype(BF16)
-    for side in range(2):
-        top, mid, low = corners[0, side], edges[side], corners[1, side]
-        line_f = jnp.concatenate([top[:, :thick], mid[:, :total], low[:, :thick]], axis=1)
-        wide = corners.shape[-1] - thick
-        over = wide - thick_a
-        line_a = jnp.concatenate(
-            [top[:, thick + over :], mid[:, total:], low[:, thick : thick + thick_a]], axis=1
-        )
-        for line, padded in ((line_f, padded_f), (line_a, padded_a)):
-            blank = jnp.zeros((LANES - EDGE, line.shape[1]), F32)
-            line = line.astype(F32)
-            if side == 0:
-                block = jnp.concatenate([blank, line], axis=0).T
-                padded[:, :LANES] = block.astype(BF16)
-            else:
-                block = jnp.concatenate([line, blank], axis=0).T
-                padded[:, LANES + cols :] = block.astype(BF16)
-
-    for padded, stack, depth in ((padded_f, stack_f, layers), (padded_a, stack_a, resps)):
-        for x in range(tall):
-            block = padded[pl.ds(x * depth, depth), :]
-            for q in range(TAPS):
-                begin = LANES - HALO + q
-                stack[pl.ds((x * TAPS + q) * depth, depth), :] = block[:, begin : begin + cols]
-
-    sampled = None
-    for h in range(rows // HALO):
-        deep = toeplitz_f.shape[1]
-        field = dot_nn(toeplitz_f[...], stack_f[pl.ds(h * HALO * TAPS * layers, deep), :])
-        high = field.astype(BF16)
-        low = (field - high.astype(F32)).astype(BF16)
-        spots = dot_nn(high, hot) + dot_nn(low, hot)
-        for a in range(HALO):
-            term = jnp.where(row_of == h * HALO + a, spots[a * resps : (a + 1) * resps], 0.0)
-            sampled = term if sampled is None else sampled + term
+        for side in range(2):
+            corner = corners[vert, side]
+            begin = thick + over if vert == 0 else thick
+            put_columns(corner[:, :thick], padded_f, start_f, side)
+            put_columns(corner[:, begin : begin + thick_a], padded_a, start_a, side)
+    shift([*range(HALO), *range(HALO + rows, tall)])
+    sampled = products([0, last], sampled)
     predicted_ref[...] = sampled * weights
-
-    for h in range(rows // HALO):
-        deep = toeplitz_a.shape[1]
-        grad = dot_nn(toeplitz_a[...], stack_a[pl.ds(h * HALO * TAPS * resps, deep), :])
-        for a in range(HALO):
-            for t in range(cols // LANES):
-                mixed[t, pl.ds(h * HALO + a, layers, stride=rows), :] = grad[
-                    a * layers : (a + 1) * layers, t * LANES : (t + 1) * LANES
-                ]
     for t in range(cols // LANES):
         gradient_ref[:, t * LANES : (t + 1) * LANES] = mixed[t]
 
 
 def fused_kernel(dims, *refs):
     arrays, results, scratch = refs[:5], refs[5:7], refs[7:]
-    exchange_kernel(dims, *arrays, *scratch[:22])
-    product_kernel(dims, *scratch[:11], *results, *scratch[22:])
+    beside, across, finish = exchange_kernel(dims, *arrays, *scratch[:22])
+    product_kernel(dims, beside, across, *scratch[:11], *results, *scratch[22:])
+    finish()
 
 
 def shards(tx_count, ty_count, model_pert, station_cells, station_resid, data_weight, kernels):

time: 21 us -> 19.4 us (0.924)
  the two profiles are of different devices: /device:TPU:0 before, /device:TPU:1 now
where the time goes in v3:
time: 19.4 us; the launch traced here: 19.2 us
  Pallas kernels  15.2 us (78%)
  local copies, waits for them, and re-layouts  3.41 us (18%)
  between operations  0.64 us (3%)
    pallas_call x1, Pallas kernels, shards(): pl.pallas_call(functools.partial(fused_kernel, dims), out_shape=(shape((r...  15.2 us
    unnamed x2, local copies, waits for them, and re-layouts  3.41 us

profile of v3, /device:TPU:1, one launch (start us, length us, event | category | flops | bytes accessed | tf_op | source)
XLA Modules:
  0.0 19.2 jit_solution(2861811187729937693)
XLA Ops:
  0.6 15.2 %shard_map.68 = (f32[48,512]{1,0:T(8,128)}, f32[512,256]{1,0:T(8,128)}) custom-call(s32[1,512]{1,0:T(1,128)} %bitcast.15, bf16[48,512]{1,0:T(8,128)(2,1)} %bitcast.14, s32[48,512]{1,0:T(8,128)} %bitcast.12, bf16[512,256]{1,0:T(8,128)(2,1)} %bitcast.11, bf16[2592,48]{1,0:T(8,128)(2,1)} %bitcast.9), custom_call_target="tpu_custom_call" | custom-call | tf_op jit(solution)/shard_map/pallas_call | solution.py:400
  15.8 1.5 %copy.9 = f32[1,1,48,512]{3,2,1,0:T(8,128)} copy(f32[1,1,48,512]{3,2,1,0:T(8,128)} %bitcast.13) | data formatting | bytes 196608
  17.3 1.9 %copy.10 = f32[32,16,256]{2,1,0:T(8,128)} copy(f32[32,16,256]{2,1,0:T(8,128)} %bitcast.10) | data formatting | bytes 1048576
